TPU v7x, 512 devices: a whole 4x4x16 slice. The times are simulated.
512 devices in a mesh: row: 64 (over x, z_lo, y), col: 8 (over z_hi, core).
Axes of the slice: x: 4, y: 4, z: 16 (z_hi: 4, z_lo: 4; z = z_hi * 4 + z_lo), core: 2. Of those that a mesh axis runs over, the one named last changes fastest.
Arguments:
- tokens: bfloat16 [320, 8192], P('row', 'col'), may hold values from -6 to 6
- cotangent: bfloat16 [320, 8192], P('row', 'col'), may hold values from -6 to 6
- gate_weight: bfloat16 [8192, 28672], P('col', 'row'), may hold values from -0.0625 to 0.0625
- up_weight: bfloat16 [8192, 28672], P('col', 'row'), may hold values from -0.0625 to 0.0625
- down_weight: bfloat16 [28672, 8192], P('row', 'col'), may hold values from -0.03125 to 0.03125
- old_in_hidden: bfloat16 [2, 8192, 128], P(None, 'col'), may hold values from -0.0625 to 0.0625
- old_out_hidden: bfloat16 [2, 128, 28672], P(None, None, 'row'), may hold values from -0.5 to 0.5
- old_in_down: bfloat16 [28672, 128], P('row'), may hold values from -0.03125 to 0.03125
- old_out_down: bfloat16 [128, 8192], P(None, 'col'), may hold values from -0.5 to 0.5
- new_in_hidden: bfloat16 [2, 8192, 128], P(None, 'col'), may hold values from -0.0625 to 0.0625
- new_in_down: bfloat16 [28672, 128], P('row'), may hold values from -0.03125 to 0.03125
- first_hidden: float32 [2, 128, 28672], P(None, 'col', 'row'), may hold values from -4 to 4
- second_hidden: float32 [2, 128, 28672], P(None, 'col', 'row'), may hold values from 0.01 to 1
- first_down: float32 [128, 8192], P('row', 'col'), may hold values from -4 to 4
- second_down: float32 [128, 8192], P('row', 'col'), may hold values from 0.01 to 1
- keep_hidden: int32 [2, 28672], P(None, 'row'), may hold values 0 or 1
- keep_down: int32 [8192], P('col'), may hold values 0 or 1
Outputs:
- input_grad: bfloat16 [320, 8192], P('row', 'col')
- new_first_hidden: float32 [2, 128, 28672], P(None, 'col', 'row')
- new_second_hidden: float32 [2, 128, 28672], P(None, 'col', 'row')
- new_first_down: float32 [128, 8192], P('row', 'col')
- new_second_down: float32 [128, 8192], P('row', 'col')
All inputs are finite; a program needn't handle non-finite values. No bound on the sum of `keep_hidden` or of `keep_down` on one device may be relied on, other than what follows from the above.
Results may differ from a plain program's by a relative error of at most 0.0072.
Values may be sent and summed in bfloat16 or wider, within the bound.
A program may use at most 64 MiB of HBM per device.

v0:
```python
import jax
import jax.numpy as jnp
from jax import lax
from jax.sharding import PartitionSpec as P

adapter_scale = 0.25


def merge_weight(frozen_weight, left, right):
    weight_increment = jnp.dot(left, right, preferred_element_type=jnp.float32)
    return (frozen_weight.astype(jnp.float32) + adapter_scale * weight_increment).astype(
        jnp.bfloat16
    )


def gate_grads(hidden_grad, gate, up):
    sig = jax.nn.sigmoid(gate)
    gate_branch_gradient = (hidden_grad * up * sig * (1.0 + gate * (1.0 - sig))).astype(
        jnp.bfloat16
    )
    up_branch_gradient = (hidden_grad * gate * sig).astype(jnp.bfloat16)
    return (gate_branch_gradient, up_branch_gradient)


def body(
    tokens,
    cotangent,
    gate_weight,
    up_weight,
    down_weight,
    old_in_hidden,
    old_out_hidden,
    old_in_down,
    old_out_down,
    new_in_hidden,
    new_in_down,
    first_hidden,
    second_hidden,
    first_down,
    second_down,
    keep_hidden,
    keep_down,
):
    merged_gate = merge_weight(gate_weight, old_in_hidden[0], old_out_hidden[0])
    merged_up = merge_weight(up_weight, old_in_hidden[1], old_out_hidden[1])
    merged_down = merge_weight(down_weight, old_in_down, old_out_down)
    width_ff = merged_gate.shape[1]
    rank = new_in_hidden.shape[2]
    rows_x, rows_dy = (
        lax.all_gather(tokens, "row", axis=0, tiled=True),
        lax.all_gather(cotangent, "row", axis=0, tiled=True),
    )
    wide = jnp.concatenate([merged_gate, merged_up, new_in_hidden[0], new_in_hidden[1]], axis=1)
    partial_value = jnp.dot(rows_x, wide, preferred_element_type=jnp.float32)
    grad_part = lax.dot_general(
        rows_dy, merged_down, (((1,), (1,)), ((), ())), preferred_element_type=jnp.float32
    )
    summed = lax.psum(partial_value, "col")
    gate = summed[:, :width_ff]
    up = summed[:, width_ff : 2 * width_ff]
    low_in = summed[:, 2 * width_ff :].astype(jnp.bfloat16)
    hidden = (gate * jax.nn.sigmoid(gate) * up).astype(jnp.bfloat16)
    hidden_grad = lax.psum(grad_part, "col")
    gate_branch_gradient, up_branch_gradient = gate_grads(hidden_grad, gate, up)
    down_part = jnp.dot(hidden, new_in_down, preferred_element_type=jnp.float32)
    down_rank_factor = lax.psum_scatter(down_part, "row", scatter_dimension=1, tiled=True).astype(
        jnp.bfloat16
    )
    both_grads = jnp.concatenate([gate_branch_gradient, up_branch_gradient], axis=1)
    both_weights = jnp.concatenate([merged_gate, merged_up], axis=1)
    input_grad = lax.psum_scatter(
        lax.dot_general(
            both_grads, both_weights, (((1,), (1,)), ((), ())), preferred_element_type=jnp.float32
        ),
        "row",
        scatter_dimension=0,
        tiled=True,
    ).astype(jnp.bfloat16)
    rank_col = rank // lax.axis_size("col")
    offset = lax.axis_index("col") * rank_col
    gate_rank_factor = lax.dynamic_slice_in_dim(low_in, offset, rank_col, 1)
    up_rank_factor = lax.dynamic_slice_in_dim(low_in, rank + offset, rank_col, 1)
    gate_adapter_gradient = adapter_scale * lax.dot_general(
        gate_rank_factor,
        gate_branch_gradient,
        (((0,), (0,)), ((), ())),
        preferred_element_type=jnp.float32,
    )
    up_adapter_gradient = adapter_scale * lax.dot_general(
        up_rank_factor,
        up_branch_gradient,
        (((0,), (0,)), ((), ())),
        preferred_element_type=jnp.float32,
    )
    grad_hidden = jnp.stack([gate_adapter_gradient, up_adapter_gradient])
    down_adapter_gradient = adapter_scale * lax.dot_general(
        down_rank_factor, rows_dy, (((0,), (0,)), ((), ())), preferred_element_type=jnp.float32
    )
    keep_h = keep_hidden.astype(jnp.float32)[:, None, :]
    keep_d = keep_down.astype(jnp.float32)[None, :]
    new_first_hidden = 0.9 * keep_h * first_hidden + 0.1 * grad_hidden
    new_second_hidden = 0.999 * keep_h * second_hidden + 0.001 * grad_hidden * grad_hidden
    new_first_down = 0.9 * keep_d * first_down + 0.1 * down_adapter_gradient
    new_second_down = (
        0.999 * keep_d * second_down + 0.001 * down_adapter_gradient * down_adapter_gradient
    )
    return (input_grad, new_first_hidden, new_second_hidden, new_first_down, new_second_down)


def solution(mesh):
    return jax.shard_map(
        body,
        mesh=mesh,
        in_specs=(
            P("row", "col"),
            P("row", "col"),
            P("col", "row"),
            P("col", "row"),
            P("row", "col"),
            P(None, "col", None),
            P(None, None, "row"),
            P("row", None),
            P(None, "col"),
            P(None, "col", None),
            P("row", None),
            P(None, "col", "row"),
            P(None, "col", "row"),
            P("row", "col"),
            P("row", "col"),
            P(None, "row"),
            P("col"),
        ),
        out_specs=(
            P("row", "col"),
            P(None, "col", "row"),
            P(None, "col", "row"),
            P("row", "col"),
            P("row", "col"),
        ),
        check_vma=False,
    )
```

profile of v0, /device:TPU:128, one launch (start us, length us, event | category | flops | bytes accessed | tf_op | source)
XLA Modules:
  0.0 929.6 jit_solution(10905582798602495780)
XLA Ops:
  7.2 0.0 copy-start
  7.2 0.0 copy-start.6
  7.2 0.0 copy-start.8
  7.2 0.0 copy-start.1
  7.2 0.0 all-reduce.7.cloned.1.call-start
  7.3 1.8 add_convert_fusion
  9.1 0.0 copy-done.6
  9.1 0.0 copy-done.8
  9.1 0.0 copy-done.1
  9.1 0.0 copy-start.2
  9.1 0.0 copy-start.7
  9.2 1.3 add_convert_fusion.1
  10.5 0.1 copy-done.7
  10.6 0.0 copy-start.11
  10.6 0.9 copy.31
  11.5 0.9 copy.32
  12.3 0.0 copy-start.12
  12.3 0.0 copy-done.11
  12.3 193.5 %all-gather.1 = bf16[64,5,1024]{2,1,0:T(8,128)(2,1)S(1)} all-gather(bf16[1,5,1024]{2,1,0:T(8,128)(2,1)S(1)} %bitcast.37), channel_id=1, replica_groups=mesh['row'=64,'col'=8] {'row'}, dimensions={0}, use_global_device_ids=true | all-gather | bytes 665600 | tf_op jit(solution)/shard_map/all_gather | solution.py:50
  205.9 0.3 reshape.21
  206.1 0.0 copy-done.12
  206.2 184.3 %all-gather = bf16[64,5,1024]{2,1,0:T(8,128)(2,1)S(1)} all-gather(bf16[1,5,1024]{2,1,0:T(8,128)(2,1)S(1)} %bitcast.38), channel_id=1, replica_groups=mesh['row'=64,'col'=8] {'row'}, dimensions={0}, use_global_device_ids=true | all-gather | bytes 665600 | tf_op jit(solution)/shard_map/all_gather | solution.py:51
  390.4 0.3 reshape.19
  390.7 0.0 copy-done
  390.7 0.0 copy-start.4
  390.7 2.9 fusion.12
  393.6 0.0 copy-done.2
  393.6 0.0 copy-done.4
  393.6 3.2 convolution_bitcast_fusion
  396.8 0.0 copy-start.15
  396.8 0.0 copy-start.16
  396.8 0.0 all-reduce.7.cloned.1.call-update
  396.9 1.3 dynamic-slice
  399.4 0.0 copy-done.15
  399.5 0.0 copy-done.16
  399.5 126.8 %all-reduce.7.cloned.1.call-done = (f32[320,448]{1,0:T(8,128)}, f32[320,1152]{1,0:T(8,128)}) async-done(((f32[320,448]{1,0:T(8,128)}, f32[320,1152]{1,0:T(8,128)}), (f32[320,448]{1,0:T(8,128)}, f32[320,1152]{1,0:T(8,128)})) %all-reduce.7.cloned.1.call-update) | async-done | bytes 2048016 | tf_op jit(solution)/shard_map/psum | solution.py:63
  526.2 0.0 copy-start.3
  526.2 0.0 copy-start.5
  526.2 1.1 slice.64
  527.4 1.9 multiply_convert_fusion.2
  529.3 0.0 copy-done.3
  529.3 0.0 copy-done.5
  529.3 0.0 copy-start.17
  529.3 0.9 fusion.7
  530.2 0.3 fusion.13
  530.4 0.3 fusion.14
  530.7 0.0 copy-done.17
  530.7 1.7 fusion.19
  532.4 0.0 copy-start.9
  532.4 0.0 copy-start.10
  532.4 0.0 copy-start.13
  532.4 0.0 copy-start.14
  532.4 388.1 %all-reduce.8 = (bf16[320,1024]{1,0:T(8,128)(2,1)S(1)}, bf16[320,128]{1,0:T(8,128)(2,1)S(1)}) all-reduce(f32[320,1024]{1,0:T(8,128)S(1)} %fusion.7, f32[320,128]{1,0:T(8,128)S(1)} %fusion.19), channel_id=2, replica_groups=mesh['row'=64,'col'=8] {'row'}, use_global_device_ids=true, to_apply=%region_2.0.clone | all-reduce | flops 368640 | bytes 2211840
  920.5 0.6 dynamic-slice_convert_fusion.2
  921.2 0.0 copy-done.9
  921.2 0.0 copy-done.10
  921.2 0.7 fusion.31
  921.8 0.0 copy-done.13
  921.8 0.0 copy-done.14
  921.8 0.9 multiply_add_fusion.1
  (3 shorter events, 0.0 us)
Async XLA Ops:
  7.2 383.5 %copy-start = (bf16[128,1024]{1,0:T(8,128)(2,1)S(1)}, bf16[128,1024]{1,0:T(8,128)(2,1)}, u32[]{:S(2)}) copy-start(bf16[128,1024]{1,0:T(8,128)(2,1)} %param.25) | copy-start | bytes 786436
  7.2 1.9 copy-start.6
  7.2 1.9 copy-start.8
  7.2 1.9 copy-start.1
  7.2 519.0 %all-reduce.7.cloned.1.call-start = ((), (), s32[]{:S(2)}) async-start(), calls=%async_computation | async-start | bytes 4259840 | tf_op jit(solution)/shard_map/psum | solution.py:63
  9.1 384.5 %copy-start.2 = (bf16[1024,448]{0,1:T(8,128)(2,1)}, bf16[1024,448]{0,1:T(8,128)(2,1)S(1)}, u32[]{:S(2)}) copy-start(bf16[1024,448]{0,1:T(8,128)(2,1)S(1)} %add_convert_fusion) | copy-start | bytes 2752516
  9.1 1.4 copy-start.7
  10.6 1.8 copy-start.11
  12.3 193.8 %copy-start.12 = (bf16[5,1024]{1,0:T(8,128)(2,1)S(1)}, bf16[5,1024]{1,0:T(8,128)(2,1)}, u32[]{:S(2)}) copy-start(bf16[5,1024]{1,0:T(8,128)(2,1)} %param.18) | copy-start | bytes 30724
  390.7 2.9 copy-start.4
  396.8 2.6 copy-start.15
  396.8 2.6 copy-start.16
  526.2 3.0 copy-start.3
  526.2 3.0 copy-start.5
  529.3 1.4 copy-start.17
  532.4 388.8 %copy-start.9 = (f32[2,16,448]{2,1,0:T(8,128)S(1)}, f32[2,16,448]{2,1,0:T(8,128)}, u32[]{:S(2)}) copy-start(f32[2,16,448]{2,1,0:T(8,128)} %param.29) | copy-start | bytes 172036
  532.4 388.8 %copy-start.10 = (f32[2,16,448]{2,1,0:T(8,128)S(1)}, f32[2,16,448]{2,1,0:T(8,128)}, u32[]{:S(2)}) copy-start(f32[2,16,448]{2,1,0:T(8,128)} %param.28) | copy-start | bytes 172036
  532.4 389.4 %copy-start.13 = (f32[2,1024]{1,0:T(2,128)S(1)}, f32[2,1024]{1,0:T(2,128)}, u32[]{:S(2)}) copy-start(f32[2,1024]{1,0:T(2,128)} %param.31) | copy-start | bytes 24580
  532.4 389.4 %copy-start.14 = (f32[2,1024]{1,0:T(2,128)S(1)}, f32[2,1024]{1,0:T(2,128)}, u32[]{:S(2)}) copy-start(f32[2,1024]{1,0:T(2,128)} %param.30) | copy-start | bytes 24580
Sparse Core Ops, SparseCore 0:
  397.0 129.2 all-reduce.6
where the time goes:
time: 930 us
  blocking collectives  766 us (82%)
  waiting for transfers between devices  127 us (14%)
  between operations  15.6 us (2%)
  matrix products  13.3 us (1%)
    unnamed x1, blocking collectives  388 us
    all_gather x1, blocking collectives, body(): lax.all_gather(tokens, 'row', axis=0, tiled=True)  194 us
    all_gather x1, blocking collectives, body(): lax.all_gather(cotangent, 'row', axis=0, tiled=True)  184 us
    psum x1, waiting for transfers between devices, body(): hidden_grad = lax.psum(grad_part, 'col')  127 us
  transfers between devices with their start and end apart: 1, of which 1 were waited for; matrix products, arithmetic and copies ran while one was open for 0% of the time, Pallas kernels for 0%

commit v1 on v0

v1 whole, which is shorter than its diff:
```python
from types import SimpleNamespace

import jax
import jax.numpy as jnp
from jax import lax
from jax.experimental import pallas as pl
from jax.experimental.pallas import tpu as pltpu
from jax.sharding import PartitionSpec as P

MESH = pl.DeviceIdType.MESH
F32 = jnp.float32
BF16 = jnp.bfloat16
SCALE = 0.25
OWNED = ((0, 3), (1, 2))
OFFSET = (0, 1, 3, 2)
SLOT = {o: q for q, o in enumerate(OFFSET)}
OWNER = {q: (k, s) for k, qs in enumerate(OWNED) for s, q in enumerate(qs)}


def dot(a, b):
    return lax.dot_general(a, b, (((1,), (0,)), ((), ())), preferred_element_type=F32)


def dot_t(a, b):
    return lax.dot_general(a, b, (((1,), (1,)), ((), ())), preferred_element_type=F32)


def one_hot(rows, cols, source):
    i = lax.broadcasted_iota(jnp.int32, (rows, cols), 0)
    j = lax.broadcasted_iota(jnp.int32, (rows, cols), 1)
    return jnp.where(source(i, j), 1.0, 0.0).astype(BF16)


SCRATCH = dict(
    w_hidden=((1024, 1024), BF16),
    w_down=((512, 1024), BF16),
    new_down_t=((4, 128, 128), BF16),
    units=((4, 16, 1024), BF16),
    quads=((4, 40, 1024), BF16),
    strip=((40, 384), BF16),
    strips=((2, 4, 40, 384), BF16),
    far_quads=((4, 40, 1024), BF16),
    left=((4, 160, 640), BF16),
    right=((4, 160, 384), BF16),
    part_send=((4, 80, 1536), BF16),
    part_recv=((4, 80, 1536), BF16),
    part=((2, 12, 80, 128), F32),
    part_b=((2, 12, 80, 128), BF16),
    relay_recv=((2, 3, 80, 128), BF16),
    relay_send=((2, 3, 80, 128), BF16),
    near_recv=((2, 3, 80, 128), BF16),
    far_recv=((2, 3, 80, 128), BF16),
    grads=((4, 4, 2, 80, 128), BF16),
    hid=((2, 80, 128), BF16),
    xy_send=((4, 4, 24, 1024), BF16),
    xy_recv=((4, 4, 24, 1024), BF16),
    z_own=((4, 8, 1024), F32),
    z_send=((4, 8, 1024), BF16),
    z_recv=((4, 8, 1024), BF16),
    d_part=((4, 32, 256), F32),
    d_xrecv=((4, 32, 256), F32),
    d_sum=((4, 8, 256), F32),
    d_zrecv=((4, 8, 256), F32),
    d_col=((8, 256), F32),
    d_crecv=((4, 8, 256), F32),
    d_both=((4, 2, 8, 256), F32),
    lt_f=((2, 4, 32, 128), F32),
    lt_b=((2, 4, 32, 128), BF16),
    lt_crecv=((4, 32, 128), BF16),
    lt_two=((4, 32, 128), F32),
    lt_two_b=((4, 32, 128), BF16),
    lt_zrecv=((4, 32, 128), BF16),
    lt=((4, 32, 128), BF16),
)
INPUTS = dict(
    tokens=(5, 1024), cotangent=(5, 1024), gate_raw=(448, 1024), up_raw=(448, 1024), down_raw=(448, 1024),
    in_raw=(2, 1024, 128), out_hidden=(2, 448, 128), in_down=(448, 128), out_down=(128, 1024),
    new_in=(2, 1024, 128), new_down=(448, 128),
)
N_SEM = 112


def kernel(*refs):
    n_in = len(INPUTS)
    ig_out, gh_out, gd_out = refs[n_in : n_in + 3]
    far = SimpleNamespace(**dict(zip(INPUTS, refs[:n_in])))
    inner = refs[n_in + 3 :]
    r = SimpleNamespace(**dict(zip(list(INPUTS) + list(SCRATCH), inner)))
    send_sem, recv_sem, local_sem = inner[n_in + len(SCRATCH) :]

    row, col = lax.axis_index("row"), lax.axis_index("col")
    x, zl, y = row // 16, lax.rem(row // 4, 4), lax.rem(row, 4)
    zh, k = col // 2, lax.rem(col, 2)

    def at(dx=0, dz=0, dy=0, dh=0, flip=False):
        to_row = lax.rem(x + dx, 4) * 16 + lax.rem(zl + dz, 4) * 4 + lax.rem(y + dy, 4)
        return (to_row, lax.rem(zh + dh, 4) * 2 + (1 - k if flip else k))

    peers = [at(dx=d) for d in (1, 2, 3)] + [at(dz=d) for d in (1, 2, 3)]
    peers += [at(dx=d, dy=e) for d in range(4) for e in (1, 2, 3)] + [at(dh=d) for d in (1, 2, 3)] + [at(flip=True)]
    barrier = pltpu.get_barrier_semaphore()
    for peer in peers:
        pl.semaphore_signal(barrier, inc=1, device_id=peer, device_id_type=MESH)

    loads = SimpleNamespace()
    for n, (name, ref) in enumerate(vars(far).items()):
        copy = pltpu.make_async_copy(ref, vars(r)[name], local_sem.at[n])
        copy.start()
        vars(loads)[name] = copy

    ids = []

    def send(src, dst, to):
        n = len(ids)
        ids.append(n)
        return pltpu.make_async_remote_copy(
            src_ref=src, dst_ref=dst, send_sem=send_sem.at[n], recv_sem=recv_sem.at[n], device_id=to, device_id_type=MESH
        )

    units = r.units
    units[zl] = jnp.zeros((16, 1024), BF16)
    loads.tokens.wait()
    loads.cotangent.wait()
    units[zl, pl.ds(0, 5), :] = r.tokens[...]
    units[zl, pl.ds(8, 5), :] = r.cotangent[...]
    pl.semaphore_wait(barrier, len(peers))
    first = [send(units.at[zl], units.at[zl], at(dz=d)) for d in (1, 2, 3)]
    for copy in first:
        copy.start()

    for copy in list(vars(loads).values())[2:]:
        copy.wait()
    w_hidden, w_down = r.w_hidden, r.w_down

    def merge_rows(n, _):
        rows = pl.ds(pl.multiple_of(n * 224, 224), 224)
        for b, raw in enumerate((r.gate_raw, r.up_raw)):
            step = dot_t(r.out_hidden[b, rows, :], r.in_raw[b])
            to = pl.ds(pl.multiple_of(b * 512 + n * 224, 32), 224)
            w_hidden[to, :] = (raw[rows, :].astype(F32) + SCALE * step).astype(BF16)
        step = dot(r.in_down[rows, :], r.out_down[...])
        w_down[rows, :] = (r.down_raw[rows, :].astype(F32) + SCALE * step).astype(BF16)
        return 0

    lax.fori_loop(0, 2, merge_rows, 0)
    for n in range(2):
        w_hidden[n * 512 + 448 : n * 512 + 512, :] = jnp.zeros((64, 1024), BF16)
    w_down[448:512, :] = jnp.zeros((64, 1024), BF16)
    for j in range(3):
        r.new_down_t[j] = r.new_down[128 * j : 128 * j + 128, :].astype(F32).T.astype(BF16)
    last = jnp.concatenate([r.new_down[384:448, :].astype(F32), jnp.zeros((64, 128), F32)], axis=0)
    r.new_down_t[3] = last.T.astype(BF16)

    for copy in first:
        copy.wait_recv()
    pick = one_hot(40, 64, lambda i, j: ((j & 7) < 5) & (i == ((j >> 3) & 1) * 20 + (j >> 4) * 5 + (j & 7)))
    quads, strip, strips, far_quads = r.quads, r.strip, r.strips, r.far_quads
    left, right = r.left, r.right
    quad = dot(pick, units[...].reshape(64, 1024)).astype(BF16)
    quads[x] = quad
    strip[...] = quad[:, 640:]
    second = [send(quads.at[x], quads.at[x], at(dx=d)) for d in (1, 2, 3)]
    over_y = [send(strip, strips.at[0, x], at(dy=3)), send(strip, strips.at[1, x], at(dy=1))]
    over_y += [send(quads.at[x], far_quads.at[x], at(dy=2))]
    for copy in second + over_y:
        copy.start()

    def arrange(get):
        total = None
        for n in range(4):
            place = one_hot(160, 40, lambda i, j, n=n: i == n * 20 + j + jnp.where(j >= 20, 60, 0))
            term = dot(place, get(n))
            total = term if total is None else total + term
        return total.astype(BF16)

    for copy in second:
        copy.wait_recv()
    chunk = arrange(lambda n: quads[n])
    left[0] = chunk[:, :640]
    right[0] = chunk[:, 640:]

    to_up = send(left.at[0], left.at[2], at(dy=1))
    to_down = send(left.at[0], left.at[1], at(dy=3))
    over_x = {
        q: [send(ref.at[x], ref.at[x], at(dx=d)) for d in (1, 2, 3)]
        for q, ref in ((1, strips.at[0]), (2, strips.at[1]), (3, far_quads))
    }
    to_up.start()
    to_down.start()
    for q in (1, 2, 3):
        over_y[q - 1].wait_recv()
        for copy in over_x[q]:
            copy.start()

    def build(q):
        if q < 3:
            (to_down, to_up)[q - 1].wait_recv()
        for copy in over_x[q]:
            copy.wait_recv()
        if q < 3:
            right[q] = arrange(lambda n: strips[q - 1, n])
        else:
            chunk = arrange(lambda n: far_quads[n])
            left[q] = chunk[:, :640]
            right[q] = chunk[:, 640:]

    def tokens(q):
        return jnp.concatenate([left[q, 0:80, :], right[q, 0:80, :]], axis=1)

    def cotangent(q):
        return jnp.concatenate([left[q, 80:160, :], right[q, 80:160, :]], axis=1)

    partner = at(flip=True)
    part_copy = {q: send(r.part_send.at[q], r.part_recv.at[q], partner) for q in range(4)}
    grads = r.grads
    grad_copy = {q: send(grads.at[q], grads.at[q], partner) for q in range(4)}
    xy_copy = {
        q: [
            send(r.xy_send.at[q, lax.rem(x + d, 4)], r.xy_recv.at[q, d], at(dx=d, dy=OFFSET[q]))
            for d in range(4)
            if q or d
        ]
        for q in range(4)
    }

    def products(q):
        for n in range(2):
            yield n * 4, dot_t(tokens(q), w_hidden[n * 512 : n * 512 + 512, :])
        yield 8, dot_t(cotangent(q), w_down[...])

    def give(q):
        for block, value in products(q):
            r.part_send[q, :, block * 128 : block * 128 + 512] = value.astype(BF16)
        part_copy[q].start()

    def keep(q):
        s = OWNER[q][1]
        for block, value in products(q):
            for b in range(4):
                r.part[s, b * 3 + block // 4] = value[:, b * 128 : b * 128 + 128]

    def groups(q):
        return ((0, 2), (2, 1)) if q in (0, 2) else ((2, 1), (0, 2))

    def ring(q):
        s = OWNER[q][1]
        (a0, an), (b0, bn) = groups(q)

        def at_j(ref, d, lo, n):
            return ref.at[s, pl.ds(lax.rem(zh + d, 4) * 3 + lo, n)]

        half = lambda ref, lo, n: ref.at[s, pl.ds(lo, n)]
        mine = r.part_b
        return SimpleNamespace(
            far_a=send(at_j(mine, 2, a0, an), half(r.relay_recv, a0, an), at(dh=1)),
            near_b=send(at_j(mine, 1, b0, bn), half(r.near_recv, b0, bn), at(dh=1)),
            far_b=send(at_j(mine, 2, b0, bn), half(r.relay_recv, b0, bn), at(dh=3)),
            near_a=send(at_j(mine, 3, a0, an), half(r.near_recv, a0, an), at(dh=3)),
            on_a=send(half(r.relay_send, a0, an), half(r.far_recv, a0, an), at(dh=1)),
            on_b=send(half(r.relay_send, b0, bn), half(r.far_recv, b0, bn), at(dh=3)),
        )

    rings = {q: ring(q) for q in range(4)}

    def reduce_start(q):
        s = OWNER[q][1]
        part_copy[q].wait_recv()
        for b in range(4):
            for c in range(3):
                lanes = c * 512 + b * 128
                total = r.part[s, b * 3 + c] + r.part_recv[q, :, lanes : lanes + 128].astype(F32)
                r.part[s, b * 3 + c] = total
                r.part_b[s, b * 3 + c] = total.astype(BF16)
        for copy in (rings[q].far_a, rings[q].far_b, rings[q].near_b, rings[q].near_a):
            copy.start()

    def reduce_relay(q):
        s = OWNER[q][1]
        for (lo, n), d, far, on in (
            (groups(q)[0], 1, rings[q].far_a, rings[q].on_a),
            (groups(q)[1], 3, rings[q].far_b, rings[q].on_b),
        ):
            far.wait_recv()
            base = lax.rem(zh + d, 4) * 3
            for c in range(lo, lo + n):
                total = r.part[s, base + c] + r.relay_recv[s, c].astype(F32)
                r.relay_send[s, c] = total.astype(BF16)
            on.start()

    def gather(q):
        here, low, high = zh, lax.rem(zh + 3, 4), lax.rem(zh + 1, 4)
        return SimpleNamespace(
            up=send(grads.at[q, here], grads.at[q, here], at(dh=1)),
            down=send(grads.at[q, here], grads.at[q, here], at(dh=3)),
            on_up=send(grads.at[q, low, pl.ds(0, 1)], grads.at[q, low, pl.ds(0, 1)], at(dh=1)),
            on_down=send(grads.at[q, high, pl.ds(1, 1)], grads.at[q, high, pl.ds(1, 1)], at(dh=3)),
        )

    gathers = {q: gather(q) for q in range(4)}

    def activate(q):
        s = OWNER[q][1]
        for copy in (rings[q].near_a, rings[q].near_b, rings[q].on_a, rings[q].on_b):
            copy.wait_recv()
        gate, up, hidden_grad = (
            r.part[s, zh * 3 + c] + r.near_recv[s, c].astype(F32) + r.far_recv[s, c].astype(F32) for c in range(3)
        )
        sig = jax.nn.sigmoid(gate)
        grads[q, zh, 0] = (hidden_grad * up * sig * (1.0 + gate * (1.0 - sig))).astype(BF16)
        grads[q, zh, 1] = (hidden_grad * gate * sig).astype(BF16)
        gathers[q].up.start()
        gathers[q].down.start()
        r.hid[s] = (gate * sig * up).astype(BF16)

    def gather_relay(q):
        gathers[q].up.wait_recv()
        gathers[q].on_up.start()
        gathers[q].down.wait_recv()
        gathers[q].on_down.start()

    def gather_end(q):
        gathers[q].on_up.wait_recv()
        gathers[q].on_down.wait_recv()
        grad_copy[q].start()

    def both(q):
        return jnp.concatenate([grads[q, j, c] for c in range(2) for j in range(4)], axis=1)

    def backward(q):
        both_grads = both(q)

        def source(i, j):
            part = jnp.where(i >= 24, 1, 0) + jnp.where(i >= 48, 1, 0) + jnp.where(i >= 72, 1, 0)
            inside = i - 24 * part
            return (inside < 20) & (j == part * 20 + inside)

        spread = one_hot(96, 80, source)
        for n in range(2):
            value = dot(both_grads, w_hidden[:, n * 512 : n * 512 + 512]).astype(BF16)
            wide = dot(spread, value).astype(BF16)
            for m in range(4):
                r.xy_send[q, m, :, n * 512 : n * 512 + 512] = wide[24 * m : 24 * m + 24]
        for copy in xy_copy[q]:
            copy.start()

    def take(q):
        grad_copy[q].wait_recv()
        backward(q)

    lt_core = send(r.lt_b.at[1 - k], r.lt_crecv, partner)
    lt_z = [send(r.lt_two_b.at[lax.rem(zh + d, 4)], r.lt_zrecv.at[d], at(dh=d)) for d in (1, 2, 3)]
    lt_y = [send(r.lt.at[0], r.lt.at[q], at(dy=(4 - OFFSET[q]) % 4)) for q in (1, 2, 3)]

    def low_start():
        for b in range(2):
            low = dot(tokens(0), r.new_in[b])
            low = jnp.concatenate([low, jnp.zeros((48, 128), F32)], axis=0).T
            for c in range(8):
                value = low[16 * c : 16 * c + 16, :]
                r.lt_f[c % 2, c // 2, 16 * b : 16 * b + 16, :] = value
                r.lt_b[c % 2, c // 2, 16 * b : 16 * b + 16, :] = value.astype(BF16)
        lt_core.start()

    def low_middle():
        lt_core.wait_recv()
        total = r.lt_f[k] + r.lt_crecv[...].astype(F32)
        r.lt_two[...] = total
        r.lt_two_b[...] = total.astype(BF16)
        for copy in lt_z:
            copy.start()

    def low_end():
        total = r.lt_two[zh]
        for d, copy in zip((1, 2, 3), lt_z):
            copy.wait_recv()
            total += r.lt_zrecv[d].astype(F32)
        r.lt[0] = total.astype(BF16)
        for copy in lt_y:
            copy.start()

    d_x = [send(r.d_part.at[lax.rem(x + d, 4)], r.d_xrecv.at[d], at(dx=d)) for d in (1, 2, 3)]
    d_z = [send(r.d_sum.at[lax.rem(zl + d, 4)], r.d_zrecv.at[d], at(dz=d)) for d in (1, 2, 3)]
    d_h = [send(r.d_col, r.d_crecv.at[d], at(dh=d)) for d in (1, 2, 3)]
    d_k = send(r.d_both.at[0, k], r.d_both.at[0, k], partner)
    d_y = [send(r.d_both.at[0], r.d_both.at[d], at(dy=4 - d)) for d in (1, 2, 3)]

    def down_x():
        for s in range(2):
            value = dot_t(r.new_down_t[zh], r.hid[s])
            value = jnp.concatenate([value, jnp.zeros((128, 48), F32)], axis=1)
            for n in range(4):
                r.d_part[n, :, s * 128 : s * 128 + 128] = value[32 * n : 32 * n + 32]
        for copy in d_x:
            copy.start()

    def down_z():
        total = r.d_part[x]
        for d, copy in zip((1, 2, 3), d_x):
            copy.wait_recv()
            total += r.d_xrecv[d]
        for n in range(4):
            r.d_sum[n] = total[8 * n : 8 * n + 8]
        for copy in d_z:
            copy.start()

    def down_h():
        total = r.d_sum[zl]
        for d, copy in zip((1, 2, 3), d_z):
            copy.wait_recv()
            total += r.d_zrecv[d]
        r.d_col[...] = total
        for copy in d_h:
            copy.start()

    def down_k():
        total = r.d_col[...]
        for d, copy in zip((1, 2, 3), d_h):
            copy.wait_recv()
            total += r.d_crecv[d]
        r.d_both[0, k] = total
        d_k.start()

    def down_y():
        d_k.wait_recv()
        for copy in d_y:
            copy.start()

    def down_end():
        for copy in d_y:
            copy.wait_recv()
        out = None
        for q in range(4):
            total = None
            for d in range(4):
                core, s = OWNER[SLOT[(OFFSET[q] - d) % 4]]
                term = r.d_both[d, core, :, s * 128 : s * 128 + 128]
                total = term if total is None else total + term
            term = dot(total[:, 0:80].astype(BF16), cotangent(q))
            out = term if out is None else out + term
        mine = out[0:2]
        for n in (1, 2, 3):
            mine = jnp.where(y == n, out[2 * n : 2 * n + 2], mine)
        gd_out[...] = SCALE * mine

    orders = (
        (
            (keep, 0), (reduce_start, 0), (low_start,), (build, 1), (give, 1), (build, 2), (give, 2), (build, 3),
            (keep, 3), (reduce_start, 3), (reduce_relay, 0), (low_middle,), (activate, 0), (reduce_relay, 3),
            (gather_relay, 0), (low_end,), (gather_end, 0), (backward, 0), (activate, 3), (down_x,), (take, 1),
            (gather_relay, 3), (down_z,), (take, 2), (gather_end, 3), (backward, 3),
        ),
        (
            (give, 0), (low_start,), (build, 1), (keep, 1), (reduce_start, 1), (build, 2), (keep, 2),
            (reduce_start, 2), (build, 3), (give, 3), (low_middle,), (reduce_relay, 1), (reduce_relay, 2),
            (activate, 1), (activate, 2), (down_x,), (low_end,), (gather_relay, 1), (gather_relay, 2), (take, 0),
            (gather_end, 1), (backward, 1), (gather_end, 2), (backward, 2), (down_z,), (take, 3),
        ),
    )
    for core in range(2):

        @pl.when(k == core)
        def _():
            for step, *args in orders[core]:
                step(*args)

    def flush(copies):
        for copy in copies:
            copy.wait_send()

    down_h()
    flush(first + second + over_y + [to_up, to_down, lt_core] + over_x[1] + over_x[2] + over_x[3] + lt_z)
    for copy in lt_y:
        copy.wait_recv()
    for b in range(2):
        out = None
        for q in range(4):
            columns = jnp.concatenate([grads[q, j, b] for j in range(4)], axis=1)
            term = dot(r.lt[q, 16 * b : 16 * b + 16, 0:80], columns)
            out = term if out is None else out + term
        gh_out[b] = SCALE * out[:, 0:448]
    for core in range(2):

        @pl.when(k == core)
        def _():
            for q in OWNED[core]:
                flush(list(vars(rings[q]).values()) + list(vars(gathers[q]).values()) + [grad_copy[q]])
            flush([part_copy[q] for q in OWNED[1 - core]])

    flush(d_x + d_z + lt_y)
    down_k()
    total = r.xy_send[0, x].astype(F32)
    for q in (0, 1, 2, 3):
        if q == 3:
            down_y()
        for copy in xy_copy[q]:
            copy.wait_recv()
        for d in range(4):
            if q or d:
                total += r.xy_recv[q, d].astype(F32)
    spread = one_hot(32, 24, lambda i, j: ((i & 7) < 5) & (j == (i >> 3) * 5 + (i & 7)))
    wide = dot(spread, total.astype(BF16))
    for n in range(4):
        r.z_own[n] = wide[8 * n : 8 * n + 8]
        r.z_send[n] = wide[8 * n : 8 * n + 8].astype(BF16)
    z_copies = [send(r.z_send.at[lax.rem(zl + d, 4)], r.z_recv.at[d], at(dz=d)) for d in (1, 2, 3)]
    for copy in z_copies:
        copy.start()
    flush(d_h + [d_k] + d_y + xy_copy[0] + xy_copy[1] + xy_copy[2] + xy_copy[3])
    down_end()
    total = r.z_own[zl]
    for d, copy in zip((1, 2, 3), z_copies):
        copy.wait_recv()
        total += r.z_recv[d].astype(F32)
    ig_out[...] = total.astype(BF16)
    flush(z_copies)


def moments(*refs):
    ins, outs, ins_v, outs_v = refs[:9], refs[9:14], refs[14:23], refs[23:28]
    in_sem, out_sem = refs[28:]
    loads = [pltpu.make_async_copy(a, b, in_sem.at[n]) for n, (a, b) in enumerate(zip(ins, ins_v))]
    stores = [pltpu.make_async_copy(a, b, out_sem.at[n]) for n, (a, b) in enumerate(zip(outs_v, outs))]
    for copy in loads:
        copy.start()
    for copy in loads:
        copy.wait()
    ig, grad_hidden, grad_down, first_hidden, second_hidden, first_down, second_down, keep_hidden, keep_down = ins_v
    outs_v[0][...] = ig[0:5, :]
    stores[0].start()
    keep = keep_hidden[...].astype(F32)
    for n in range(2):
        kept = jnp.broadcast_to(keep[n : n + 1, :], (16, 448))
        grad = grad_hidden[n]
        outs_v[1][n] = 0.9 * kept * first_hidden[n] + 0.1 * grad
        outs_v[2][n] = 0.999 * kept * second_hidden[n] + 0.001 * grad * grad
    stores[1].start()
    stores[2].start()
    kept = jnp.broadcast_to(keep_down[...].astype(F32), (2, 1024))
    grad = grad_down[...]
    outs_v[3][...] = 0.9 * kept * first_down[...] + 0.1 * grad
    outs_v[4][...] = 0.999 * kept * second_down[...] + 0.001 * grad * grad
    stores[3].start()
    stores[4].start()
    for copy in stores:
        copy.wait()


def body(
    tokens, cotangent, gate_weight, up_weight, down_weight, old_in_hidden, old_out_hidden, old_in_down,
    old_out_down, new_in_hidden, new_in_down, first_hidden, second_hidden, first_down, second_down,
    keep_hidden, keep_down,
):
    vmem = pl.BlockSpec(memory_space=pltpu.VMEM)
    far = pl.BlockSpec(memory_space=pltpu.HBM)
    ig, grad_hidden, grad_down = pl.pallas_call(
        kernel,
        out_shape=(
            jax.ShapeDtypeStruct((8, 1024), BF16),
            jax.ShapeDtypeStruct((2, 16, 448), F32),
            jax.ShapeDtypeStruct((2, 1024), F32),
        ),
        in_specs=[far] * len(INPUTS),
        out_specs=(vmem, vmem, vmem),
        scratch_shapes=[pltpu.VMEM(shape, BF16) for shape in INPUTS.values()]
        + [pltpu.VMEM(*spec) for spec in SCRATCH.values()]
        + [pltpu.SemaphoreType.DMA((N_SEM,)), pltpu.SemaphoreType.DMA((N_SEM,)), pltpu.SemaphoreType.DMA((len(INPUTS),))],
        compiler_params=pltpu.CompilerParams(
            collective_id=0, has_side_effects=True, vmem_limit_bytes=63 * 2**20
        ),
        cost_estimate=pl.CostEstimate(flops=2_000_000_000, bytes_accessed=4_000_000, transcendentals=150_000),
        name="layer",
    )(
        tokens, cotangent, gate_weight.T, up_weight.T, down_weight, old_in_hidden, old_out_hidden.transpose(0, 2, 1),
        old_in_down, old_out_down, new_in_hidden, new_in_down,
    )
    sources = (
        ig, grad_hidden, grad_down, first_hidden, second_hidden, first_down, second_down, keep_hidden,
        keep_down.reshape(1, 1024),
    )
    results = (
        jax.ShapeDtypeStruct((5, 1024), BF16),
        jax.ShapeDtypeStruct((2, 16, 448), F32),
        jax.ShapeDtypeStruct((2, 16, 448), F32),
        jax.ShapeDtypeStruct((2, 1024), F32),
        jax.ShapeDtypeStruct((2, 1024), F32),
    )
    return pl.pallas_call(
        moments,
        out_shape=results,
        in_specs=[far] * len(sources),
        out_specs=[far] * len(results),
        scratch_shapes=[pltpu.VMEM(a.shape, a.dtype) for a in sources + results]
        + [pltpu.SemaphoreType.DMA((len(sources),)), pltpu.SemaphoreType.DMA((len(results),))],
        compiler_params=pltpu.CompilerParams(vmem_limit_bytes=63 * 2**20),
        name="moments",
    )(*sources)


def solution(mesh):
    return jax.shard_map(
        body,
        mesh=mesh,
        in_specs=(
            P("row", "col"), P("row", "col"), P("col", "row"), P("col", "row"), P("row", "col"),
            P(None, "col", None), P(None, None, "row"), P("row", None), P(None, "col"), P(None, "col", None),
            P("row", None), P(None, "col", "row"), P(None, "col", "row"), P("row", "col"), P("row", "col"),
            P(None, "row"), P("col"),
        ),
        out_specs=(
            P("row", "col"), P(None, "col", "row"), P(None, "col", "row"), P("row", "col"), P("row", "col"),
        ),
        check_vma=False,
    )
```

time: 930 us -> 94.1 us (0.10)
  the two profiles are of different devices: /device:TPU:128 before, /device:TPU:1 now
where the time goes in v1:
time: 94.1 us; the launch traced here: 93.8 us
  Pallas kernels  93.1 us (99%)
    pallas_call x1, Pallas kernels, body(): pl.pallas_call(kernel, out_shape=(jax.ShapeDtypeStruct((8, 1024), BF16),...  91.4 us

profile of v1, /device:TPU:1, one launch (start us, length us, event | category | flops | bytes accessed | tf_op | source)
XLA Modules:
  0.0 93.8 jit_solution(12359335614890734192)
XLA Ops:
  0.6 91.4 %layer.1 = (bf16[8,1024]{1,0:T(8,128)(2,1)}, f32[2,16,448]{2,1,0:T(8,128)}, f32[2,1024]{1,0:T(2,128)}) custom-call(bf16[5,1024]{1,0:T(8,128)(2,1)} %refs_0_.1, bf16[5,1024]{1,0:T(8,128)(2,1)} %refs_1_.1, bf16[448,1024]{1,0:T(8,128)(2,1)} %bitcast.5, bf16[448,1024]{1,0:T(8,128)(2,1)} %bitcast.6, bf16[448,1024]{1,0:T(8,128)(2,1)} %refs_4_.2, ...), custom_call_target="tpu_custom_call" | custom-call | flops 2000000000 | bytes 4000000 | tf_op jit(solution)/shard_map/layer/pallas_call | solution.py:555
  92.0 1.7 %moments.1 = (bf16[5,1024]{1,0:T(8,128)(2,1)}, f32[2,16,448]{2,1,0:T(8,128)}, f32[2,16,448]{2,1,0:T(8,128)}, f32[2,1024]{1,0:T(2,128)}, f32[2,1024]{1,0:T(2,128)}) custom-call(bf16[8,1024]{1,0:T(8,128)(2,1)} %get-tuple-element.8.refs_0_, f32[2,16,448]{2,1,0:T(8,128)} %get-tuple-element.9.refs_1_, f32[2,1024]{1,0:T(2,128)} %get-tuple-element.10.refs_2_, ...), custom_call_target="tpu_custom_call" | custom-call | tf_op jit(solution)/shard_map/moments/pallas_call | solution.py:587

commit v2 on v1

--- a/solution.py
+++ b/solution.py
@@ -37,11 +37,11 @@
     new_down_t=((4, 128, 128), BF16),
     units=((4, 16, 1024), BF16),
     quads=((4, 40, 1024), BF16),
-    strip=((40, 384), BF16),
-    strips=((2, 4, 40, 384), BF16),
+    strip=((40, 512), BF16),
+    strips=((2, 4, 40, 512), BF16),
     far_quads=((4, 40, 1024), BF16),
-    left=((4, 160, 640), BF16),
-    right=((4, 160, 384), BF16),
+    left=((4, 160, 512), BF16),
+    right=((4, 160, 512), BF16),
     part_send=((4, 80, 1536), BF16),
     part_recv=((4, 80, 1536), BF16),
     part=((2, 12, 80, 128), F32),
@@ -67,9 +67,12 @@
     lt_f=((2, 4, 32, 128), F32),
     lt_b=((2, 4, 32, 128), BF16),
     lt_crecv=((4, 32, 128), BF16),
-    lt_two=((4, 32, 128), F32),
-    lt_two_b=((4, 32, 128), BF16),
-    lt_zrecv=((4, 32, 128), BF16),
+    lt_two=((4, 2, 16, 128), F32),
+    lt_two_b=((4, 2, 16, 128), BF16),
+    lt_relay_recv=((2, 16, 128), BF16),
+    lt_relay_send=((2, 16, 128), BF16),
+    lt_near=((2, 16, 128), BF16),
+    lt_far=((2, 16, 128), BF16),
     lt=((4, 32, 128), BF16),
 )
 INPUTS = dict(
@@ -97,7 +100,7 @@
         return (to_row, lax.rem(zh + dh, 4) * 2 + (1 - k if flip else k))
 
     peers = [at(dx=d) for d in (1, 2, 3)] + [at(dz=d) for d in (1, 2, 3)]
-    peers += [at(dx=d, dy=e) for d in range(4) for e in (1, 2, 3)] + [at(dh=d) for d in (1, 2, 3)] + [at(flip=True)]
+    peers += [at(dx=d, dy=e) for d in range(4) for e in (1, 2, 3)] + [at(dh=d) for d in (1, 3)] + [at(flip=True)]
     barrier = pltpu.get_barrier_semaphore()
     for peer in peers:
         pl.semaphore_signal(barrier, inc=1, device_id=peer, device_id_type=MESH)
@@ -158,7 +161,7 @@
     left, right = r.left, r.right
     quad = dot(pick, units[...].reshape(64, 1024)).astype(BF16)
     quads[x] = quad
-    strip[...] = quad[:, 640:]
+    strip[...] = quad[:, 512:]
     second = [send(quads.at[x], quads.at[x], at(dx=d)) for d in (1, 2, 3)]
     over_y = [send(strip, strips.at[0, x], at(dy=3)), send(strip, strips.at[1, x], at(dy=1))]
     over_y += [send(quads.at[x], far_quads.at[x], at(dy=2))]
@@ -176,8 +179,8 @@
     for copy in second:
         copy.wait_recv()
     chunk = arrange(lambda n: quads[n])
-    left[0] = chunk[:, :640]
-    right[0] = chunk[:, 640:]
+    left[0] = chunk[:, :512]
+    right[0] = chunk[:, 512:]
 
     to_up = send(left.at[0], left.at[2], at(dy=1))
     to_down = send(left.at[0], left.at[1], at(dy=3))
@@ -201,8 +204,8 @@
             right[q] = arrange(lambda n: strips[q - 1, n])
         else:
             chunk = arrange(lambda n: far_quads[n])
-            left[q] = chunk[:, :640]
-            right[q] = chunk[:, 640:]
+            left[q] = chunk[:, :512]
+            right[q] = chunk[:, 512:]
 
     def tokens(q):
         return jnp.concatenate([left[q, 0:80, :], right[q, 0:80, :]], axis=1)
@@ -348,7 +351,10 @@
         backward(q)
 
     lt_core = send(r.lt_b.at[1 - k], r.lt_crecv, partner)
-    lt_z = [send(r.lt_two_b.at[lax.rem(zh + d, 4)], r.lt_zrecv.at[d], at(dh=d)) for d in (1, 2, 3)]
+    lt_shard = lambda d, half: r.lt_two_b.at[lax.rem(zh + d, 4), half]
+    lt_first = [send(lt_shard(2, half), r.lt_relay_recv.at[half], at(dh=(1, 3)[half])) for half in range(2)]
+    lt_first += [send(lt_shard((3, 1)[half], half), r.lt_near.at[half], at(dh=(3, 1)[half])) for half in range(2)]
+    lt_second = [send(r.lt_relay_send.at[half], r.lt_far.at[half], at(dh=(1, 3)[half])) for half in range(2)]
     lt_y = [send(r.lt.at[0], r.lt.at[q], at(dy=(4 - OFFSET[q]) % 4)) for q in (1, 2, 3)]
 
     def low_start():
@@ -363,24 +369,35 @@
 
     def low_middle():
         lt_core.wait_recv()
-        total = r.lt_f[k] + r.lt_crecv[...].astype(F32)
-        r.lt_two[...] = total
-        r.lt_two_b[...] = total.astype(BF16)
-        for copy in lt_z:
-            copy.start()
+        for j in range(4):
+            for half in range(2):
+                rows = slice(16 * half, 16 * half + 16)
+                total = r.lt_f[k, j, rows, :] + r.lt_crecv[j, rows, :].astype(F32)
+                r.lt_two[j, half] = total
+                r.lt_two_b[j, half] = total.astype(BF16)
+        for copy in lt_first:
+            copy.start()
+
+    def low_relay():
+        for half in range(2):
+            lt_first[half].wait_recv()
+            total = r.lt_two[lax.rem(zh + (1, 3)[half], 4), half] + r.lt_relay_recv[half].astype(F32)
+            r.lt_relay_send[half] = total.astype(BF16)
+            lt_second[half].start()
 
     def low_end():
-        total = r.lt_two[zh]
-        for d, copy in zip((1, 2, 3), lt_z):
-            copy.wait_recv()
-            total += r.lt_zrecv[d].astype(F32)
-        r.lt[0] = total.astype(BF16)
+        for half in range(2):
+            lt_first[2 + half].wait_recv()
+            lt_second[half].wait_recv()
+            total = r.lt_two[zh, half] + r.lt_near[half].astype(F32) + r.lt_far[half].astype(F32)
+            r.lt[0, 16 * half : 16 * half + 16, :] = total.astype(BF16)
         for copy in lt_y:
             copy.start()
 
     d_x = [send(r.d_part.at[lax.rem(x + d, 4)], r.d_xrecv.at[d], at(dx=d)) for d in (1, 2, 3)]
     d_z = [send(r.d_sum.at[lax.rem(zl + d, 4)], r.d_zrecv.at[d], at(dz=d)) for d in (1, 2, 3)]
-    d_h = [send(r.d_col, r.d_crecv.at[d], at(dh=d)) for d in (1, 2, 3)]
+    d_h = [send(r.d_col, r.d_crecv.at[d], at(dh=d)) for d in (1, 3)]
+    d_h += [send(r.d_crecv.at[1], r.d_crecv.at[2], at(dh=1))]
     d_k = send(r.d_both.at[0, k], r.d_both.at[0, k], partner)
     d_y = [send(r.d_both.at[0], r.d_both.at[d], at(dy=4 - d)) for d in (1, 2, 3)]
 
@@ -409,14 +426,17 @@
             copy.wait_recv()
             total += r.d_zrecv[d]
         r.d_col[...] = total
-        for copy in d_h:
-            copy.start()
+        d_h[0].start()
+        d_h[1].start()
+
+    def down_relay():
+        d_h[0].wait_recv()
+        d_h[2].start()
 
     def down_k():
-        total = r.d_col[...]
-        for d, copy in zip((1, 2, 3), d_h):
-            copy.wait_recv()
-            total += r.d_crecv[d]
+        d_h[1].wait_recv()
+        d_h[2].wait_recv()
+        total = r.d_col[...] + r.d_crecv[1] + r.d_crecv[2] + r.d_crecv[3]
         r.d_both[0, k] = total
         d_k.start()
 
@@ -444,14 +464,14 @@
 
     orders = (
         (
-            (keep, 0), (reduce_start, 0), (low_start,), (build, 1), (give, 1), (build, 2), (give, 2), (build, 3),
-            (keep, 3), (reduce_start, 3), (reduce_relay, 0), (low_middle,), (activate, 0), (reduce_relay, 3),
-            (gather_relay, 0), (low_end,), (gather_end, 0), (backward, 0), (activate, 3), (down_x,), (take, 1),
-            (gather_relay, 3), (down_z,), (take, 2), (gather_end, 3), (backward, 3),
+            (keep, 0), (reduce_start, 0), (low_start,), (low_middle,), (build, 1), (give, 1), (reduce_relay, 0),
+            (build, 2), (give, 2), (build, 3), (keep, 3), (reduce_start, 3), (low_relay,), (activate, 0),
+            (reduce_relay, 3), (gather_relay, 0), (low_end,), (gather_end, 0), (backward, 0), (activate, 3), (down_x,),
+            (take, 1), (gather_relay, 3), (down_z,), (take, 2), (gather_end, 3), (backward, 3),
         ),
         (
-            (give, 0), (low_start,), (build, 1), (keep, 1), (reduce_start, 1), (build, 2), (keep, 2),
-            (reduce_start, 2), (build, 3), (give, 3), (low_middle,), (reduce_relay, 1), (reduce_relay, 2),
+            (give, 0), (low_start,), (low_middle,), (build, 1), (keep, 1), (reduce_start, 1), (build, 2), (keep, 2),
+            (reduce_start, 2), (build, 3), (give, 3), (low_relay,), (reduce_relay, 1), (reduce_relay, 2),
             (activate, 1), (activate, 2), (down_x,), (low_end,), (gather_relay, 1), (gather_relay, 2), (take, 0),
             (gather_end, 1), (backward, 1), (gather_end, 2), (backward, 2), (down_z,), (take, 3),
         ),
@@ -468,7 +488,8 @@
             copy.wait_send()
 
     down_h()
-    flush(first + second + over_y + [to_up, to_down, lt_core] + over_x[1] + over_x[2] + over_x[3] + lt_z)
+    flush(first + second + over_y + [to_up, to_down, lt_core] + over_x[1] + over_x[2] + over_x[3])
+    flush(lt_first + lt_second)
     for copy in lt_y:
         copy.wait_recv()
     for b in range(2):
@@ -487,10 +508,11 @@
             flush([part_copy[q] for q in OWNED[1 - core]])
 
     flush(d_x + d_z + lt_y)
-    down_k()
+    down_relay()
     total = r.xy_send[0, x].astype(F32)
     for q in (0, 1, 2, 3):
         if q == 3:
+            down_k()
             down_y()
         for copy in xy_copy[q]:
             copy.wait_recv()

time: 94.1 us -> 90.8 us (0.965)
  Pallas kernels: 93.1 us -> 89.8 us
    pallas_call x1, Pallas kernels: 91.4 us -> 88.1 us  [body(): pl.pallas_call(kernel, out_shape=(jax.ShapeDtypeStruct((8, 1024), BF16),...]
where the time goes in v2:
time: 90.8 us; the launch traced here: 90.5 us
  Pallas kernels  89.8 us (99%)
    pallas_call x1, Pallas kernels, body(): pl.pallas_call(kernel, out_shape=(jax.ShapeDtypeStruct((8, 1024), BF16),...  88.1 us

profile of v2, /device:TPU:1, one launch (start us, length us, event | category | flops | bytes accessed | tf_op | source)
XLA Modules:
  0.0 90.5 jit_solution(4966201006276454822)
XLA Ops:
  0.6 88.1 %layer.1 = (bf16[8,1024]{1,0:T(8,128)(2,1)}, f32[2,16,448]{2,1,0:T(8,128)}, f32[2,1024]{1,0:T(2,128)}) custom-call(bf16[5,1024]{1,0:T(8,128)(2,1)} %refs_0_.1, bf16[5,1024]{1,0:T(8,128)(2,1)} %refs_1_.1, bf16[448,1024]{1,0:T(8,128)(2,1)} %bitcast.5, bf16[448,1024]{1,0:T(8,128)(2,1)} %bitcast.6, bf16[448,1024]{1,0:T(8,128)(2,1)} %refs_4_.2, ...), custom_call_target="tpu_custom_call" | custom-call | flops 2000000000 | bytes 4000000 | tf_op jit(solution)/shard_map/layer/pallas_call | solution.py:577
  88.7 1.7 %moments.1 = (bf16[5,1024]{1,0:T(8,128)(2,1)}, f32[2,16,448]{2,1,0:T(8,128)}, f32[2,16,448]{2,1,0:T(8,128)}, f32[2,1024]{1,0:T(2,128)}, f32[2,1024]{1,0:T(2,128)}) custom-call(bf16[8,1024]{1,0:T(8,128)(2,1)} %get-tuple-element.8.refs_0_, f32[2,16,448]{2,1,0:T(8,128)} %get-tuple-element.9.refs_1_, f32[2,1024]{1,0:T(2,128)} %get-tuple-element.10.refs_2_, ...), custom_call_target="tpu_custom_call" | custom-call | tf_op jit(solution)/shard_map/moments/pallas_call | solution.py:609

commit v3 on v2

--- a/solution.py
+++ b/solution.py
@@ -467,13 +467,13 @@
             (keep, 0), (reduce_start, 0), (low_start,), (low_middle,), (build, 1), (give, 1), (reduce_relay, 0),
             (build, 2), (give, 2), (build, 3), (keep, 3), (reduce_start, 3), (low_relay,), (activate, 0),
             (reduce_relay, 3), (gather_relay, 0), (low_end,), (gather_end, 0), (backward, 0), (activate, 3), (down_x,),
-            (take, 1), (gather_relay, 3), (down_z,), (take, 2), (gather_end, 3), (backward, 3),
+            (gather_relay, 3), (down_z,), (take, 1), (take, 2), (down_h,), (gather_end, 3), (backward, 3),
         ),
         (
             (give, 0), (low_start,), (low_middle,), (build, 1), (keep, 1), (reduce_start, 1), (build, 2), (keep, 2),
             (reduce_start, 2), (build, 3), (give, 3), (low_relay,), (reduce_relay, 1), (reduce_relay, 2),
-            (activate, 1), (activate, 2), (down_x,), (low_end,), (gather_relay, 1), (gather_relay, 2), (take, 0),
-            (gather_end, 1), (backward, 1), (gather_end, 2), (backward, 2), (down_z,), (take, 3),
+            (activate, 1), (activate, 2), (down_x,), (low_end,), (gather_relay, 1), (gather_relay, 2), (down_z,), (take, 0),
+            (gather_end, 1), (backward, 1), (down_h,), (gather_end, 2), (backward, 2), (take, 3),
         ),
     )
     for core in range(2):
@@ -487,7 +487,6 @@
         for copy in copies:
             copy.wait_send()
 
-    down_h()
     flush(first + second + over_y + [to_up, to_down, lt_core] + over_x[1] + over_x[2] + over_x[3])
     flush(lt_first + lt_second)
     for copy in lt_y:

time: 90.8 us -> 90.5 us (level)
  no operation moved by 1% of the time
where the time goes in v3:
time: 90.5 us; the launch traced here: 90.2 us
  Pallas kernels  89.6 us (99%)
    pallas_call x1, Pallas kernels, body(): pl.pallas_call(kernel, out_shape=(jax.ShapeDtypeStruct((8, 1024), BF16),...  87.8 us

profile of v3, /device:TPU:1, one launch (start us, length us, event | category | flops | bytes accessed | tf_op | source)
XLA Modules:
  0.0 90.2 jit_solution(17914465586128732014)
XLA Ops:
  0.6 87.8 %layer.1 = (bf16[8,1024]{1,0:T(8,128)(2,1)}, f32[2,16,448]{2,1,0:T(8,128)}, f32[2,1024]{1,0:T(2,128)}) custom-call(bf16[5,1024]{1,0:T(8,128)(2,1)} %refs_0_.1, bf16[5,1024]{1,0:T(8,128)(2,1)} %refs_1_.1, bf16[448,1024]{1,0:T(8,128)(2,1)} %bitcast.5, bf16[448,1024]{1,0:T(8,128)(2,1)} %bitcast.6, bf16[448,1024]{1,0:T(8,128)(2,1)} %refs_4_.2, ...), custom_call_target="tpu_custom_call" | custom-call | flops 2000000000 | bytes 4000000 | tf_op jit(solution)/shard_map/layer/pallas_call | solution.py:576
  88.5 1.7 %moments.1 = (bf16[5,1024]{1,0:T(8,128)(2,1)}, f32[2,16,448]{2,1,0:T(8,128)}, f32[2,16,448]{2,1,0:T(8,128)}, f32[2,1024]{1,0:T(2,128)}, f32[2,1024]{1,0:T(2,128)}) custom-call(bf16[8,1024]{1,0:T(8,128)(2,1)} %get-tuple-element.8.refs_0_, f32[2,16,448]{2,1,0:T(8,128)} %get-tuple-element.9.refs_1_, f32[2,1024]{1,0:T(2,128)} %get-tuple-element.10.refs_2_, ...), custom_call_target="tpu_custom_call" | custom-call | tf_op jit(solution)/shard_map/moments/pallas_call | solution.py:608
